TPU v7x, 256 devices: a whole 4x4x8 slice. The times are simulated.
256 devices in a mesh: rep: 8 (over y, z_hi), ep: 32 (over x, z_lo, core).
Axes of the slice: x: 4, y: 4, z: 8 (z_hi: 2, z_lo: 4; z = z_hi * 4 + z_lo), core: 2. Of those that a mesh axis runs over, the one named last changes fastest.
Arguments:
- out_grad: bfloat16 [65536, 3584], P(('rep', 'ep')), may hold values from -0.8984375 to 0.8984375
- expert_ids: int32 [65536, 8], P(('rep', 'ep')), may hold values from 0 to 255, as said below
- slots: int32 [65536, 8], P(('rep', 'ep')), may hold values from -1 to 11, as said below
- gate_weights: bfloat16 [65536, 8], P(('rep', 'ep')), may hold values from 0.049804688 to 0.59765625
- saved_gate_up: bfloat16 [8, 32, 384, 2048], P('rep', 'ep'), may hold values from -6 to 6
- master: float32 [32, 1024, 3584], P('ep', 'rep'), may hold values from -0.1875 to 0.1875
- moment1: bfloat16 [32, 1024, 3584], P('ep', 'rep'), may hold values from -0.59765625 to 0.59765625
- moment2: bfloat16 [32, 1024, 3584], P('ep', 'rep'), may hold values from 0.0009994507 to 0.0099487305
Outputs:
- grad_gate_up: bfloat16 [8, 32, 384, 2048], P('rep', 'ep')
- gate_grad: float32 [65536, 8], P(('rep', 'ep'))
- master_out: float32 [32, 1024, 3584], P('ep', 'rep')
- moment1_out: bfloat16 [32, 1024, 3584], P('ep', 'rep')
- moment2_out: bfloat16 [32, 1024, 3584], P('ep', 'rep')
Inputs may be any that keep to these rules, and one draw needn't show every extreme that they name: `expert_ids`: each row names 8 different experts of 0 to 255. Within the rows of one device, the choices naming one expert, taken in order of token then choice, have slots 0, 1, 2 and so on; those from 12 on are -1. Every device has an expert of the window with more than 12 such choices.
All inputs are finite; a program needn't handle non-finite values.
Results may differ from a plain program's by a relative error of at most 0.025.
Values may be sent and summed in bfloat16 or wider, within the bound.
A program may use at most 128 MiB of HBM per device.

v0:
```python
import jax
import jax.numpy as jnp
from jax import lax
from jax.sharding import PartitionSpec as P

TOPK = 8
EXP_LOCAL = 8
SEND = 12


beta_one = 0.9
beta_two = 0.95
learn_rate = 0.002
decay_rate = 0.1
adam_eps = 1e-08
adam_step = 50


def swiglu_backward(gate_up, weights, grad_proj):
    half_width = gate_up.shape[-1] // 2
    gate_part = gate_up[..., :half_width].astype(jnp.float32)
    up_part = gate_up[..., half_width:].astype(jnp.float32)
    sigmoid_gate = jax.nn.sigmoid(gate_part)
    silu_gate = gate_part * sigmoid_gate
    hidden = lax.optimization_barrier((silu_gate * up_part).astype(jnp.bfloat16))
    scale = weights.astype(jnp.float32)[..., None]
    scaled = (scale * hidden.astype(jnp.float32)).astype(jnp.bfloat16)
    grad_hidden = scale * grad_proj
    d_gate = grad_hidden * up_part * sigmoid_gate * (1.0 + gate_part * (1.0 - sigmoid_gate))
    d_up = grad_hidden * silu_gate
    return (hidden, scaled, jnp.concatenate([d_gate, d_up], axis=-1).astype(jnp.bfloat16))


def adamw(master, moment1, moment2, grad):
    m_new = beta_one * moment1.astype(jnp.float32) + (1.0 - beta_one) * grad
    v_new = beta_two * moment2.astype(jnp.float32) + (1.0 - beta_two) * grad * grad
    corr_one = 1.0 - beta_one**adam_step
    corr_two = 1.0 - beta_two**adam_step
    update = m_new / corr_one / (jnp.sqrt(v_new / corr_two) + adam_eps)
    master_new = master - learn_rate * (update + decay_rate * master)
    return (master_new, m_new.astype(jnp.bfloat16), v_new.astype(jnp.bfloat16))


def per_device(out_grad, expert_ids, slots, gate_weights, saved_gate_up, master, moment1, moment2):
    ep_size = lax.axis_size("ep")
    tok_rows = out_grad.shape[0]
    width = out_grad.shape[1]
    filled = ep_size * SEND
    live = (expert_ids % EXP_LOCAL == 0) & (slots >= 0)
    position = jnp.where(live, expert_ids // EXP_LOCAL * SEND + slots, filled)
    flat_pos = position.reshape(-1)
    token_of = jnp.broadcast_to(
        jnp.arange(tok_rows, dtype=jnp.int32)[:, None], position.shape
    ).reshape(-1)
    source_row = jnp.full((filled + 1,), tok_rows, jnp.int32).at[flat_pos].set(token_of)[:filled]
    padded = jnp.concatenate([out_grad, jnp.zeros((1, width), out_grad.dtype)], axis=0)
    send_rows = padded[source_row].reshape(ep_size, SEND, width)
    send_weights = (
        jnp.zeros((filled + 1,), gate_weights.dtype).at[flat_pos].set(gate_weights.reshape(-1))
    )
    send_weights = send_weights[:filled].reshape(ep_size, SEND)
    recv_rows, recv_weights = (
        lax.all_to_all(send_rows, "ep", split_axis=0, concat_axis=0, tiled=True),
        lax.all_to_all(send_weights, "ep", split_axis=0, concat_axis=0, tiled=True),
    )
    dout = recv_rows.reshape(filled, width)
    slot_weight = recv_weights.reshape(filled)
    full_weight = lax.all_gather(master[0].astype(jnp.bfloat16), "rep", axis=0, tiled=True)
    grad_proj = lax.dot_general(
        dout, full_weight, (((1,), (1,)), ((), ())), preferred_element_type=jnp.float32
    )
    gate_up = saved_gate_up[0, 0]
    hidden, scaled, grad_gate_up = swiglu_backward(gate_up, slot_weight, grad_proj)
    grad = lax.psum_scatter(
        lax.dot_general(
            scaled, dout, (((0,), (0,)), ((), ())), preferred_element_type=jnp.float32
        ).astype(jnp.bfloat16),
        "rep",
        scatter_dimension=0,
        tiled=True,
    ).astype(jnp.float32)
    master_out, moment1_out, moment2_out = adamw(master, moment1, moment2, grad[None])
    expert_out = jnp.dot(hidden, full_weight, preferred_element_type=jnp.float32).astype(
        jnp.bfloat16
    )
    back_rows = lax.all_to_all(
        expert_out.reshape(ep_size, SEND, width), "ep", split_axis=0, concat_axis=0, tiled=True
    )
    back_pad = jnp.concatenate(
        [back_rows.reshape(filled, width), jnp.zeros((1, width), jnp.bfloat16)], axis=0
    )
    grad_f = out_grad.astype(jnp.float32)
    scores = [
        jnp.sum(grad_f * back_pad[position[:, which]].astype(jnp.float32), axis=-1)
        for which in range(TOPK)
    ]
    gate_grad = jnp.stack(scores, axis=1)
    gate_grad = jnp.where(live, gate_grad, jnp.zeros((), jnp.float32))
    return (
        grad_gate_up.reshape(saved_gate_up.shape),
        gate_grad,
        master_out,
        moment1_out,
        moment2_out,
    )


def solution(mesh):
    in_specs = (
        P(("rep", "ep"), None),
        P(("rep", "ep"), None),
        P(("rep", "ep"), None),
        P(("rep", "ep"), None),
        P("rep", "ep", None, None),
        P("ep", "rep", None),
        P("ep", "rep", None),
        P("ep", "rep", None),
    )
    out_specs = (
        P("rep", "ep", None, None),
        P(("rep", "ep"), None),
        P("ep", "rep", None),
        P("ep", "rep", None),
        P("ep", "rep", None),
    )
    return jax.shard_map(
        per_device, mesh=mesh, in_specs=in_specs, out_specs=out_specs, check_vma=False
    )
```

profile of v0, /device:TPU:1, one launch (start us, length us, event | category | flops | bytes accessed | tf_op | source)
XLA Modules:
  0.0 632.2 jit_solution(9630475385744545462)
XLA Ops:
  7.2 0.8 copy.16
  8.0 0.1 reshape.192
  8.1 0.7 fusion.38
  8.8 0.1 copy.15
  9.0 0.1 reshape.108
  9.1 14.6 %scatter_custom_fusion = bf16[385]{0:T(512)(128)(2,1)S(1)} fusion(s32[2048]{0:T(1024)S(1)} %bitcast.57, bf16[2048]{0:T(1024)(128)(2,1)S(1)} %reshape.192, bf16[]{:T(256)} %constant.22.clone.1), kind=kCustom, calls=%fused_computation.98 | custom fusion | bytes 772 | tf_op jit(solution)/shard_map/scatter | solution.py:59
  23.7 0.7 all_to_all.16
  24.4 10.0 %all-to-all-start = ((bf16[32,1,12]{2,1,0:T(2,128)(2,1)}), bf16[32,1,12]{2,1,0:T(2,128)(2,1)S(1)}, u32[]{:S(2)}, u32[]{:S(2)}) async-start(bf16[32,1,12]{2,1,0:T(2,128)(2,1)} %all_to_all.16), calls=%async_computation | async-start | bytes 32768 | tf_op jit(solution)/shard_map/all_to_all | solution.py:64
  34.5 0.1 reshape.200
  34.6 8.0 %scatter_custom_fusion.1 = s32[385]{0:T(512)S(1)} fusion(s32[2048]{0:T(1024)S(1)} %bitcast.58, s32[2048]{0:T(1024)S(1)} %reshape.200, s32[]{:T(128)} %constant.56.clone.1), kind=kCustom, calls=%fused_computation.96 | custom fusion | bytes 1544 | tf_op jit(solution)/shard_map/scatter | solution.py:55
  42.6 1.6 concatenate.21
  44.3 3.9 gather_fusion
  48.1 5.3 reshape.111
  53.5 0.0 copy-start
  53.5 0.0 all-to-all-done
  53.5 7.9 %all-to-all-start.1 = ((bf16[32,12,3584]{2,1,0:T(8,128)(2,1)}), bf16[32,12,3584]{2,1,0:T(8,128)(2,1)}, u32[]{:S(2)}, u32[]{:S(2)}) async-start(bf16[32,12,3584]{2,1,0:T(8,128)(2,1)} %reshape.111), calls=%async_computation.1 | async-start | bytes 7340032 | tf_op jit(solution)/shard_map/all_to_all | solution.py:63
  61.3 0.0 reduce-scatter.2.cloned.1.call-start
  61.4 0.0 copy-done
  61.4 0.5 fusion.22
  61.9 0.1 convert_reduce_fusion
  62.0 0.1 reshape.115
  62.1 82.6 %all-to-all-done.1 = bf16[32,12,3584]{2,1,0:T(8,128)(2,1)} async-done(((bf16[32,12,3584]{2,1,0:T(8,128)(2,1)}), bf16[32,12,3584]{2,1,0:T(8,128)(2,1)}, u32[]{:S(2)}, u32[]{:S(2)}) %all-to-all-start.1) | async-done | bytes 2752544 | tf_op jit(solution)/shard_map/all_to_all | solution.py:63
  144.6 3.8 reshape.112
  148.4 6.2 convolution_convert_fusion
  154.7 0.0 reduce-scatter.2.cloned.1.call-update
  154.7 0.2 all-gather.3.cloned.1.call-start
  154.9 170.8 %reduce-scatter.2.cloned.1.call-done = bf16[128,3584]{1,0:T(8,128)(2,1)} async-done(((bf16[1024,3584]{1,0:T(8,128)(2,1)}), bf16[128,3584]{1,0:T(8,128)(2,1)}) %reduce-scatter.2.cloned.1.call-update) | async-done | bytes 917520 | tf_op jit(solution)/shard_map/reduce_scatter | solution.py:74
  325.7 7.1 %fusion.30 = (bf16[1,128,3584]{2,1,0:T(8,128)(2,1)}, f32[1,128,3584]{2,1,0:T(8,128)}, bf16[1,128,3584]{2,1,0:T(8,128)(2,1)}, bf16[1,128,3584]{2,1,0:T(8,128)(2,1)}) fusion(bf16[128,3584]{1,0:T(8,128)(2,1)} %reduce-scatter.2.cloned.1.call-done, bf16[1,128,3584]{2,1,0:T(8,128)(2,1)} %param.15, f32[1,128,3584]{2,1,0:T(8,128)} %param.13, ...), kind=kLoop, calls=%fused_computation.57 | loop fusion | flops 9633792 | bytes 9175040 | tf_op jit(solution)/shard_map/convert_element_type | solution.py:41
  332.7 0.0 all-gather.3.cloned.1.call-update
  332.8 151.8 %all-gather.3.cloned.1.call-done = bf16[1,1024,3584]{2,1,0:T(8,128)(2,1)} async-done(((bf16[1,128,3584]{2,1,0:T(8,128)(2,1)}), bf16[1,1024,3584]{2,1,0:T(8,128)(2,1)}) %all-gather.3.cloned.1.call-update) | async-done | bytes 7340048 | tf_op jit(solution)/shard_map/all_gather | solution.py:68
  484.6 7.4 %fusion.4 = bf16[384,3584]{1,0:T(8,128)(2,1)} fusion(bf16[384,1024]{1,0:T(8,128)(2,1)S(1)} %fusion.22, bf16[1,1024,3584]{2,1,0:T(8,128)(2,1)} %all-gather.3.cloned.1.call-done), kind=kOutput, calls=%fused_computation.24 | convolution fusion | flops 2819948544 | bytes 10878976 | tf_op jit(solution)/shard_map/dot_general | solution.py:83
  492.0 5.3 reshape.113
  497.3 5.6 all-to-all-start.2
  503.0 6.9 %fusion.34 = (bf16[1,1,384,1024]{3,2,1,0:T(8,128)(2,1)S(1)}, bf16[1,1,384,1024]{3,2,1,0:T(8,128)(2,1)S(1)}) fusion(bf16[384,2048]{1,0:T(8,128)(2,1)} %bitcast.55, bf16[384,3584]{1,0:T(8,128)(2,1)S(1)} %reshape.112, bf16[1,1024,3584]{2,1,0:T(8,128)(2,1)} %all-gather.3.cloned.1.call-done, f32[384]{0:T(512)S(1)} %reshape.115), kind=kOutput, calls=%fused_computation.61 | convolution fusion | flops 2824863744 | bytes 13239808 | tf_op jit(solution)/shard_map/dot_general | solution.py:69
  510.0 1.3 pad_maximum_fusion
  511.3 75.0 %all-to-all-done.2 = bf16[32,12,3584]{2,1,0:T(8,128)(2,1)} async-done(((bf16[32,12,3584]{2,1,0:T(8,128)(2,1)}), bf16[32,12,3584]{2,1,0:T(8,128)(2,1)}, u32[]{:S(2)}, u32[]{:S(2)}) %all-to-all-start.2) | async-done | bytes 2752544 | tf_op jit(solution)/shard_map/all_to_all | solution.py:86
  586.2 5.3 reshape.114
  591.6 2.0 concatenate.25
  593.5 3.0 gather_fusion.8
  596.5 3.0 gather_fusion.7
  599.4 3.0 gather_fusion.6
  602.4 3.0 gather_fusion.5
  605.5 3.0 gather_fusion.4
  608.5 3.0 gather_fusion.3
  611.4 2.9 gather_fusion.2
  614.4 3.0 gather_fusion.1
  617.4 0.0 copy-start.1
  617.4 0.0 copy-start.2
  617.4 7.3 %fusion.14 = (f32[256]{0:T(256)S(1)}, f32[256]{0:T(256)S(1)}, f32[256]{0:T(256)S(1)}, f32[256]{0:T(256)S(1)}, f32[256]{0:T(256)S(1)}, /*index=5*/f32[256]{0:T(256)S(1)}, f32[256]{0:T(256)S(1)}, f32[256]{0:T(256)S(1)}) fusion(bf16[256,3584]{1,0:T(8,128)(2,1)} %param.8, bf16[256,3584]{1,0:T(8,128)(2,1)} %gather_fusion.8, bf16[256,3584]{1,0:T(8,128)(2,1)} %gather_fusion.2, ...), kind=kLoop, calls=%fused_computation.32 | loop fusion | flops 22935552 | bytes 16523264 | tf_op jit(solution)/shard_map/reduce_sum | solution.py:94
  624.7 0.0 copy-done.1
  624.7 0.0 copy-done.2
  624.7 0.6 broadcast_select_fusion
  (14 shorter events, 0.1 us)
Async XLA Ops:
  24.4 29.1 %all-to-all-start = ((bf16[32,1,12]{2,1,0:T(2,128)(2,1)}), bf16[32,1,12]{2,1,0:T(2,128)(2,1)S(1)}, u32[]{:S(2)}, u32[]{:S(2)}) async-start(bf16[32,1,12]{2,1,0:T(2,128)(2,1)} %all_to_all.16), calls=%async_computation | async-start | bytes 32768 | tf_op jit(solution)/shard_map/all_to_all | solution.py:64
  53.5 7.9 %copy-start = (bf16[1,1,384,2048]{3,2,1,0:T(8,128)(2,1)S(1)}, bf16[1,1,384,2048]{3,2,1,0:T(8,128)(2,1)}, u32[]{:S(2)}) copy-start(bf16[1,1,384,2048]{3,2,1,0:T(8,128)(2,1)} %param.12) | copy-start | bytes 4718596
  53.5 91.2 %all-to-all-start.1 = ((bf16[32,12,3584]{2,1,0:T(8,128)(2,1)}), bf16[32,12,3584]{2,1,0:T(8,128)(2,1)}, u32[]{:S(2)}, u32[]{:S(2)}) async-start(bf16[32,12,3584]{2,1,0:T(8,128)(2,1)} %reshape.111), calls=%async_computation.1 | async-start | bytes 7340032 | tf_op jit(solution)/shard_map/all_to_all | solution.py:63
  61.3 264.3 %reduce-scatter.2.cloned.1.call-start = ((), (), s32[]{:S(2)}) async-start(), calls=%async_computation.4 | async-start | bytes 8257536 | tf_op jit(solution)/shard_map/reduce_scatter | solution.py:74
  154.7 329.9 %all-gather.3.cloned.1.call-start = ((), (), s32[]{:S(2)}) async-start(), calls=%async_computation.5 | async-start | bytes 8257536 | tf_op jit(solution)/shard_map/all_gather | solution.py:68
  497.3 88.9 %all-to-all-start.2 = ((bf16[32,12,3584]{2,1,0:T(8,128)(2,1)}), bf16[32,12,3584]{2,1,0:T(8,128)(2,1)}, u32[]{:S(2)}, u32[]{:S(2)}) async-start(bf16[32,12,3584]{2,1,0:T(8,128)(2,1)} %reshape.113), calls=%async_computation.2 | async-start | bytes 7340032 | tf_op jit(solution)/shard_map/all_to_all | solution.py:86
  617.4 7.3 %copy-start.1 = (s32[256,8]{0,1:T(8,128)S(1)}, s32[256,8]{0,1:T(8,128)}, u32[]{:S(2)}) copy-start(s32[256,8]{0,1:T(8,128)} %param.10) | copy-start | bytes 24580
  617.4 7.3 %copy-start.2 = (s32[256,8]{0,1:T(8,128)S(1)}, s32[256,8]{0,1:T(8,128)}, u32[]{:S(2)}) copy-start(s32[256,8]{0,1:T(8,128)} %param.9) | copy-start | bytes 24580
Sparse Core Ops, SparseCore 0:
  154.8 170.8 reduce-scatter.1
  332.9 151.6 all-gather.2
where the time goes:
time: 633 us; the launch traced here: 632 us
  waiting for transfers between devices  480 us (76%)
  local copies, waits for them, and re-layouts  75.8 us (12%)
  starting transfers between devices  23.7 us (4%)
  matrix products  20.6 us (3%)
  other arithmetic  17.6 us (3%)
  between operations  14.3 us (2%)
    reduce_scatter x1, waiting for transfers between devices, per_device(): lax.psum_scatter(lax.dot_general(scaled, dout, (((0,), (0,)), ((), ())),...  171 us
    all_gather x1, waiting for transfers between devices, per_device(): lax.all_gather(master[0].astype(jnp.bfloat16), 'rep', axis=0, tiled=True)  152 us
    all_to_all x1, waiting for transfers between devices, per_device(): lax.all_to_all(send_rows, 'ep', split_axis=0, concat_axis=0, tiled=True)  82.6 us
    all_to_all x1, waiting for transfers between devices, per_device(): lax.all_to_all(expert_out.reshape(ep_size, SEND, width), 'ep', split_axis...  75 us
    gather x8, local copies, waits for them, and re-layouts, per_device(): back_pad[position[:, which]].astype(jnp.float32)  23.8 us
    scatter x1, local copies, waits for them, and re-layouts, per_device(): jnp.zeros((filled + 1,), gate_weights.dtype).at[flat_pos]  14.6 us
  transfers between devices with their start and end apart: 5, of which 4 were waited for; matrix products, arithmetic and copies ran while one was open for 4% of the time, Pallas kernels for 0%

commit v1 on v0

v1 whole, which is shorter than its diff:
```python
import functools

import jax
import jax.numpy as jnp
from jax import lax
from jax.experimental import pallas as pl
from jax.experimental.pallas import tpu as pltpu
from jax.sharding import PartitionSpec as P

TOPK = 8
EXP_LOCAL = 8
SEND = 12
PARTS = 4
CHUNKS = (3, 4)
TILE = 512
MESH = pl.DeviceIdType.MESH

beta_one = 0.9
beta_two = 0.95
learn_rate = 0.002
decay_rate = 0.1
adam_eps = 1e-08
adam_step = 50


def adamw(master, moment1, moment2, grad):
    m_new = beta_one * moment1.astype(jnp.float32) + (1.0 - beta_one) * grad
    v_new = beta_two * moment2.astype(jnp.float32) + (1.0 - beta_two) * grad * grad
    corr_one = 1.0 - beta_one**adam_step
    corr_two = 1.0 - beta_two**adam_step
    update = m_new / corr_one / (jnp.sqrt(v_new / corr_two) + adam_eps)
    master_new = master - learn_rate * (update + decay_rate * master)
    return (master_new, m_new.astype(jnp.bfloat16), v_new.astype(jnp.bfloat16))


def iota(shape, dim):
    return lax.broadcasted_iota(jnp.int32, shape, dim)


def div(x, by, top):
    shift = 20
    factor = (1 << shift) // by + 1
    assert all((v * factor) >> shift == v // by for v in range(top)) and top * factor < 2**31
    return (x * factor) >> shift


def kernel(
    n_ep, n_rep,
    ids_ref, slots_ref, gates_ref, og_hbm, gu_hbm, master_hbm,
    ggu_out, gate_out, grad_out,
    og, gu, master, pick, unpick,
    rows_out, rows_in, w_out, w_in, dout, wcol,
    hidden, d_silu, silu, scaled_t, shards,
    s1, r1, keep, s2own, r2own, s2sum, r2sum, own, zs, zr,
    gg_acc, gg_out, gg_in,
    load_sem, rows_ssem, rows_rsem, small_ssem, small_rsem, local_sem, ssem, rsem,
):
    f32, bf16 = jnp.float32, jnp.bfloat16
    r, e = lax.axis_index("rep"), lax.axis_index("ep")
    y, h = lax.div(r, 2), lax.rem(r, 2)
    n_y = n_rep // 2
    up = (lax.rem(r + 2, n_rep), e)
    down = (lax.rem(r + n_rep - 2, n_rep), e)
    across = (r + 1 - 2 * h, e)
    width = og.shape[1]
    part_rows = shards.shape[0] // n_rep
    pair = 2 * part_rows
    msg = PARTS * SEND
    offsets = [sum(CHUNKS[:i]) * PARTS * 128 for i in range(len(CHUNKS))]

    def peer(k):
        return lax.rem(e + k, n_ep)

    loads = [
        pltpu.make_async_copy(src, dst, load_sem.at[i])
        for i, (src, dst) in enumerate(((og_hbm, og), (master_hbm, master), (gu_hbm, gu)))
    ]
    for load in loads:
        load.start()

    barrier = pltpu.get_barrier_semaphore()

    def greet(k, _):
        pl.semaphore_signal(barrier, inc=1, device_id=(r, peer(k)), device_id_type=MESH)
        return _

    lax.fori_loop(1, n_ep, greet, 0)
    for other in (up, down, across):
        pl.semaphore_signal(barrier, inc=1, device_id=other, device_id_type=MESH)

    ids, slots = ids_ref[...], slots_ref[...]
    live = ((ids & (EXP_LOCAL - 1)) == 0) & (slots >= 0)
    expert = ids >> 3
    pos12 = jnp.where(live, expert * SEND + slots, -64)
    pos16 = jnp.where(live, expert * 16 + slots, -64)
    gates = gates_ref[...]
    n_tok = ids.shape[1]

    def weight_rows(b, _):
        row = iota((64, n_tok), 0) + b * 64
        total = jnp.zeros((64, n_tok), f32)
        for k in range(TOPK):
            total += jnp.where(row == pos16[k : k + 1, :], gates[k : k + 1, :], 0.0)
        column = jnp.sum(total, axis=1, keepdims=True)
        w_out[pl.ds(pl.multiple_of(b * 64, 64), 64), :] = jnp.broadcast_to(column, (64, 128)).astype(bf16)
        return _

    lax.fori_loop(0, n_ep * 16 // 64, weight_rows, 0)

    def pick_rows(g, _):
        row = iota((PARTS * msg, n_tok), 0)
        dest = div(row, msg, PARTS * msg)
        rest = row - dest * msg
        part = div(rest, SEND, msg)
        target = (dest + g * PARTS) * SEND + rest - part * SEND
        hit = target == pos12[0:1, :]
        for k in range(1, TOPK):
            hit = hit | (target == pos12[k : k + 1, :])
        for q in range(PARTS):
            one = jnp.where(hit & (part == q), 1.0, 0.0).astype(bf16)
            pick[pl.ds(pl.multiple_of(g * PARTS * msg, 16), PARTS * msg), q * n_tok : (q + 1) * n_tok] = one
        return _

    lax.fori_loop(0, n_ep // PARTS, pick_rows, 0)

    mine = pl.ds(pl.multiple_of(r * part_rows, part_rows), part_rows)
    loads[1].wait()

    def cast(t, _):
        cols = pl.ds(pl.multiple_of(t * TILE, TILE), TILE)
        shards[mine, cols] = master[:, cols].astype(bf16)
        return _

    lax.fori_loop(0, width // TILE, cast, 0)

    def remote(src, dst, i, other):
        return pltpu.make_async_remote_copy(
            src_ref=src, dst_ref=dst, send_sem=ssem.at[i], recv_sem=rsem.at[i],
            device_id=other, device_id_type=MESH,
        )

    pl.semaphore_wait(barrier, n_ep - 1 + 3)

    def shard(rep):
        return shards.at[pl.ds(pl.multiple_of(rep * part_rows, part_rows), part_rows)]

    def half_shard(rep, which):
        half = part_rows // 2
        return shards.at[pl.ds(pl.multiple_of(rep * part_rows + which * half, half), half)]

    started = []

    def start(copy):
        copy.start()
        started.append(copy)
        return copy

    ag_up = start(remote(shard(r), shard(r), 0, up))
    ag_down = start(remote(shard(r), shard(r), 1, down))

    def small(src_of, dst, rows, sems):
        def send(k, _):
            to = peer(k)
            pltpu.make_async_remote_copy(
                src_ref=src_of(to), dst_ref=dst.at[pl.ds(pl.multiple_of(e * rows, rows), rows)],
                send_sem=small_ssem.at[sems], recv_sem=small_rsem.at[sems],
                device_id=(r, to), device_id_type=MESH,
            ).start()
            return _

        lax.fori_loop(1, n_ep, send, 0)
        copy = pltpu.make_async_copy(
            src_of(e), dst.at[pl.ds(pl.multiple_of(e * rows, rows), rows)], local_sem.at[sems]
        )
        copy.start()
        return copy

    def all_of(ref, rows, sem):
        part = ref.at[pl.ds(0, (n_ep - 1) * rows)]
        return pltpu.make_async_copy(part, part, sem)

    w_local = small(lambda to: w_out.at[pl.ds(pl.multiple_of(to * 16, 16), 16)], w_in, 16, 0)

    loads[0].wait()
    rows_local = []
    for p, size in enumerate(CHUNKS):
        wide = size * 128
        out, into = rows_out[p], rows_in[p]

        def gather(g, _, out=out, wide=wide, p=p):
            where = pl.ds(pl.multiple_of(g * PARTS * msg, 16), PARTS * msg)
            total = jnp.zeros((PARTS * msg, wide), f32)
            for q in range(PARTS):
                total += jnp.dot(
                    pick[where, q * n_tok : (q + 1) * n_tok],
                    og[:, offsets[p] + q * wide : offsets[p] + (q + 1) * wide],
                    preferred_element_type=f32,
                )
            out[where, :] = total.astype(bf16)
            return _

        lax.fori_loop(0, n_ep // PARTS, gather, 0)

        def block(ref, i):
            return ref.at[pl.ds(pl.multiple_of(i * msg, 16), msg)]

        def send(k, _, out=out, into=into, p=p):
            to = peer(k)
            pltpu.make_async_remote_copy(
                src_ref=block(out, to), dst_ref=block(into, e),
                send_sem=rows_ssem.at[p], recv_sem=rows_rsem.at[p],
                device_id=(r, to), device_id_type=MESH,
            ).start()
            return _

        lax.fori_loop(1, n_ep, send, 0)
        copy = pltpu.make_async_copy(block(out, e), block(into, e), local_sem.at[2 + p])
        copy.start()
        rows_local.append(copy)

    loads[2].wait()
    n_hidden = hidden.shape[1]
    step = 128

    def activation(t, _):
        cols = pl.ds(pl.multiple_of(t * step, step), step)
        up_cols = pl.ds(pl.multiple_of(n_hidden + t * step, step), step)
        gate, lift = gu[:, cols].astype(f32), gu[:, up_cols].astype(f32)
        sig = jax.nn.sigmoid(gate)
        act = gate * sig
        hidden[:, cols] = (act * lift).astype(bf16)
        silu[:, cols] = act
        d_silu[:, cols] = lift * sig * (1.0 + gate * (1.0 - sig))
        return _

    lax.fori_loop(0, n_hidden // step, activation, 0)
    side = PARTS * msg
    row = iota((side, side), 0)
    part = div(row, msg, side)
    rest = row - part * msg
    dest = div(rest, SEND, msg)
    unpick[...] = jnp.where(
        iota((side, side), 1) == dest * msg + part * SEND + rest - dest * SEND, 1.0, 0.0
    ).astype(bf16)

    w_local.wait()
    all_of(w_in, 16, small_rsem.at[0]).wait()
    n_slots = n_ep * SEND
    row = iota((n_slots, n_ep * 16), 0)
    dest = div(row, SEND, n_slots)
    order = jnp.where(iota(row.shape, 1) == row + dest * (16 - SEND), 1.0, 0.0).astype(bf16)
    wcol[...] = jnp.dot(order, w_in[...], preferred_element_type=f32)

    def scale(t, _):
        cols = pl.ds(pl.multiple_of(t * step, step), step)
        value = wcol[...] * hidden[:, cols].astype(f32)
        scaled_t[cols, :] = value.astype(bf16).astype(f32).T.astype(bf16)
        return _

    lax.fori_loop(0, n_hidden // step, scale, 0)

    ag_up.wait_recv()
    ag_up2 = start(remote(half_shard(down[0], 0), half_shard(down[0], 0), 2, up))
    ag_down.wait_recv()
    ag_down2 = start(remote(half_shard(up[0], 1), half_shard(up[0], 1), 3, down))

    def span(p):
        return pl.ds(offsets[p], CHUNKS[p] * PARTS * 128)

    def tiles(p, body):
        def one(t, _):
            body(pl.ds(pl.multiple_of(offsets[p] + t * TILE, TILE), TILE))
            return _

        lax.fori_loop(0, CHUNKS[p] * PARTS * 128 // TILE, one, 0)

    def arrive(p):
        wide = CHUNKS[p] * 128
        rows_local[p].wait()
        all_of(rows_in[p], msg, rows_rsem.at[p]).wait()

        def restore(g, _):
            got = jnp.dot(
                unpick[...],
                rows_in[p][pl.ds(pl.multiple_of(g * side, 16), side), :],
                preferred_element_type=f32,
            ).astype(bf16)
            for q in range(PARTS):
                dout[pl.ds(pl.multiple_of(g * msg, 16), msg), offsets[p] + q * wide : offsets[p] + (q + 1) * wide] = (
                    got[q * msg : (q + 1) * msg]
                )
            return _

        lax.fori_loop(0, n_ep // PARTS, restore, 0)

    def product(to_y, cols):
        rows = pl.ds(pl.multiple_of(to_y * pair, pair), pair)
        return jnp.dot(scaled_t[rows, :], dout[:, cols], preferred_element_type=f32)

    y_up, y_down, y_far = lax.rem(y + 1, n_y), lax.rem(y + n_y - 1, n_y), lax.rem(y + 2, n_y)
    first, second = pl.ds(0, part_rows), pl.ds(part_rows, part_rows)
    base = 9
    flights = {}

    def stage_one(p):
        def far(cols):
            s1[:, cols] = product(y_far, cols).astype(bf16)

        tiles(p, far)
        i = base + 7 * p
        flights[p, "a"] = start(remote(s1.at[first, span(p)], r1.at[first, span(p)], i, up))
        flights[p, "b"] = start(remote(s1.at[second, span(p)], r1.at[second, span(p)], i + 1, down))

        def near(cols):
            got = product(y_up, cols)
            keep[first, cols] = got[:part_rows]
            s2own[second, cols] = got[part_rows:].astype(bf16)
            got = product(y_down, cols)
            s2own[first, cols] = got[:part_rows].astype(bf16)
            keep[second, cols] = got[part_rows:]

        tiles(p, near)
        flights[p, "own_b"] = start(remote(s2own.at[second, span(p)], r2own.at[second, span(p)], i + 2, up))
        flights[p, "own_a"] = start(remote(s2own.at[first, span(p)], r2own.at[first, span(p)], i + 3, down))

        def here(cols):
            own[:, cols] = product(y, cols)

        tiles(p, here)

    def stage_two(p):
        i = base + 7 * p
        for name, rows, other, j in (("a", first, up, i + 4), ("b", second, down, i + 5)):
            flights[p, name].wait_recv()

            def add(cols, rows=rows):
                s2sum[rows, cols] = (keep[rows, cols] + r1[rows, cols].astype(f32)).astype(bf16)

            tiles(p, add)
            flights[p, "sum_" + name] = start(remote(s2sum.at[rows, span(p)], r2sum.at[rows, span(p)], j, other))

    def stage_three(p):
        for name in ("own_a", "own_b", "sum_a", "sum_b"):
            flights[p, name].wait_recv()

        def half(which, cols):
            rows = pl.ds(pl.multiple_of(which * part_rows, part_rows), part_rows)
            return own[rows, cols] + (r2own[rows, cols].astype(f32) + r2sum[rows, cols].astype(f32))

        def other(cols):
            zs[:, cols] = half(1 - h, cols).astype(bf16)

        tiles(p, other)
        flights[p, "z"] = start(remote(zs.at[:, span(p)], zr.at[:, span(p)], base + 7 * p + 6, across))

        def mine_too(cols):
            grad_out[:, cols] = half(h, cols)

        tiles(p, mine_too)

    def stage_four(p):
        flights[p, "z"].wait_recv()

        def finish(cols):
            grad_out[:, cols] = grad_out[:, cols] + zr[:, cols].astype(f32)

        tiles(p, finish)

    m_step = 128

    def gate_part(to_y):
        rows = pl.ds(pl.multiple_of(to_y * pair, pair), pair)
        cols = rows
        up_cols = pl.ds(pl.multiple_of(n_hidden + to_y * pair, pair), pair)

        def block(m, _):
            where = pl.ds(pl.multiple_of(m * m_step, m_step), m_step)
            proj = lax.dot_general(
                dout[where, :], shards[rows, :], (((1,), (1,)), ((), ())), preferred_element_type=f32
            )
            felt = hidden[where, cols].astype(f32) * proj
            total = gg_acc[where, :]
            for c in range(pair // 128):
                total = total + felt[:, c * 128 : (c + 1) * 128]
            gg_acc[where, :] = total
            grad_hidden = wcol[where, 0:1] * proj
            ggu_out[where, cols] = (grad_hidden * d_silu[where, cols]).astype(bf16)
            ggu_out[where, up_cols] = (grad_hidden * silu[where, cols]).astype(bf16)
            return _

        lax.fori_loop(0, n_slots // m_step, block, 0)

    gg_acc[...] = jnp.zeros_like(gg_acc)

    arrive(0)
    stage_one(0)
    ag_z = start(remote(shard(r), shard(r), 4, across))
    stage_two(0)
    arrive(1)
    stage_one(1)
    stage_three(0)
    stage_two(1)

    ag_z.wait_recv()
    ag_up3 = start(remote(shard(across[0]), shard(across[0]), 5, up))
    ag_down3 = start(remote(shard(across[0]), shard(across[0]), 6, down))
    stage_three(1)
    gate_part(y)
    up_other, down_other = across[0] + 2, across[0] + n_rep - 2
    up_other, down_other = lax.rem(up_other, n_rep), lax.rem(down_other, n_rep)
    ag_up3.wait_recv()
    ag_up4 = start(remote(half_shard(down_other, 0), half_shard(down_other, 0), 7, up))
    ag_down3.wait_recv()
    ag_down4 = start(remote(half_shard(up_other, 1), half_shard(up_other, 1), 8, down))
    gate_part(y_down)
    gate_part(y_up)
    stage_four(0)
    for copy in (ag_up2, ag_down2, ag_up4, ag_down4):
        copy.wait_recv()
    gate_part(y_far)

    gg_out[...] = jnp.broadcast_to(jnp.sum(gg_acc[...], axis=1, keepdims=True), gg_out.shape)

    def window(to):
        return gg_out.at[pl.ds(pl.multiple_of(to * SEND - 4 * lax.rem(to, 2), 8), 16)]

    gg_local = small(window, gg_in, 16, 1)
    stage_four(1)
    gg_local.wait()
    all_of(gg_in, 16, small_rsem.at[1]).wait()
    row = iota((n_ep * 16, 128), 0) - 4 * lax.rem(e, 2)
    back = gg_in[...]
    for k in range(TOPK):
        for b in range(n_tok // 128):
            cols = slice(b * 128, (b + 1) * 128)
            hit = row == pos16[k : k + 1, cols]
            gate_out[k : k + 1, cols] = jnp.sum(jnp.where(hit, back, 0.0), axis=0, keepdims=True)

    for copy in started:
        copy.wait_send()
    all_of(w_out, 16, small_ssem.at[0]).wait()
    all_of(gg_in, 16, small_ssem.at[1]).wait()
    for p in range(len(CHUNKS)):
        all_of(rows_out[p], msg, rows_ssem.at[p]).wait()


def outer(
    n_ep, n_rep,
    ids_ref, slots_ref, gates_ref, og_hbm, gu_hbm, master_hbm,
    ggu_out, gate_out, grad_out, *scratch,
):
    n = len(CHUNKS)
    og, gu, master, pick, unpick = scratch[:5]
    rows_out, rows_in = scratch[5 : 5 + n], scratch[5 + n : 5 + 2 * n]
    kernel(
        n_ep, n_rep, ids_ref, slots_ref, gates_ref, og_hbm, gu_hbm, master_hbm,
        ggu_out, gate_out, grad_out,
        og, gu, master, pick, unpick, rows_out, rows_in, *scratch[5 + 2 * n :],
    )


def exchange(n_ep, n_rep, ids, slots, gates, out_grad, gate_up, master):
    tokens, width = out_grad.shape
    n_slots, two_hidden = gate_up.shape
    n_hidden = two_hidden // 2
    part_rows = master.shape[0]
    pair = 2 * part_rows
    msg = PARTS * SEND
    f32, bf16 = jnp.float32, jnp.bfloat16
    n = len(CHUNKS)
    n_sems = 9 + 7 * n
    vmem = pl.BlockSpec(memory_space=pltpu.VMEM)
    hbm = pl.BlockSpec(memory_space=pl.ANY)
    rows = [pltpu.VMEM((n_ep * msg, size * 128), bf16) for size in CHUNKS]
    dma = pltpu.SemaphoreType.DMA
    return pl.pallas_call(
        functools.partial(outer, n_ep, n_rep),
        out_shape=(
            jax.ShapeDtypeStruct((n_slots, two_hidden), bf16),
            jax.ShapeDtypeStruct((TOPK, tokens), f32),
            jax.ShapeDtypeStruct((part_rows, width), f32),
        ),
        in_specs=[vmem, vmem, vmem, hbm, hbm, hbm],
        out_specs=(vmem, vmem, vmem),
        scratch_shapes=[
            pltpu.VMEM((tokens, width), bf16),
            pltpu.VMEM((n_slots, two_hidden), bf16),
            pltpu.VMEM((part_rows, width), f32),
            pltpu.VMEM((n_ep * msg, PARTS * tokens), bf16),
            pltpu.VMEM((PARTS * msg, PARTS * msg), bf16),
            *rows,
            *rows,
            pltpu.VMEM((n_ep * 16, 128), bf16),
            pltpu.VMEM((n_ep * 16, 128), bf16),
            pltpu.VMEM((n_slots, width), bf16),
            pltpu.VMEM((n_slots, 128), f32),
            pltpu.VMEM((n_slots, n_hidden), bf16),
            pltpu.VMEM((n_slots, n_hidden), f32),
            pltpu.VMEM((n_slots, n_hidden), f32),
            pltpu.VMEM((n_hidden, n_slots), bf16),
            pltpu.VMEM((n_hidden, width), bf16),
            pltpu.VMEM((pair, width), bf16),
            pltpu.VMEM((pair, width), bf16),
            pltpu.VMEM((pair, width), f32),
            pltpu.VMEM((pair, width), bf16),
            pltpu.VMEM((pair, width), bf16),
            pltpu.VMEM((pair, width), bf16),
            pltpu.VMEM((pair, width), bf16),
            pltpu.VMEM((pair, width), f32),
            pltpu.VMEM((part_rows, width), bf16),
            pltpu.VMEM((part_rows, width), bf16),
            pltpu.VMEM((n_slots, 128), f32),
            pltpu.VMEM((n_slots, 128), f32),
            pltpu.VMEM((n_ep * 16, 128), f32),
            dma((3,)),
            dma((n,)),
            dma((n,)),
            dma((2,)),
            dma((2,)),
            dma((2 + n,)),
            dma((n_sems,)),
            dma((n_sems,)),
        ],
        compiler_params=pltpu.CompilerParams(
            collective_id=0, has_side_effects=True, vmem_limit_bytes=60 * 1024 * 1024
        ),
        name="exchange",
    )(ids, slots, gates, out_grad, gate_up, master)


def solution(mesh):
    n_ep, n_rep = mesh.shape["ep"], mesh.shape["rep"]

    def per_device(out_grad, expert_ids, slots, gate_weights, saved_gate_up, master, moment1, moment2):
        grad_gate_up, gate_grad, grad = exchange(
            n_ep, n_rep, expert_ids.T, slots.T, gate_weights.T.astype(jnp.float32),
            out_grad, saved_gate_up[0, 0], master[0],
        )
        master_out, moment1_out, moment2_out = adamw(master, moment1, moment2, grad[None])
        return (grad_gate_up.reshape(saved_gate_up.shape), gate_grad.T, master_out, moment1_out, moment2_out)

    in_specs = (
        P(("rep", "ep"), None),
        P(("rep", "ep"), None),
        P(("rep", "ep"), None),
        P(("rep", "ep"), None),
        P("rep", "ep", None, None),
        P("ep", "rep", None),
        P("ep", "rep", None),
        P("ep", "rep", None),
    )
    out_specs = (
        P("rep", "ep", None, None),
        P(("rep", "ep"), None),
        P("ep", "rep", None),
        P("ep", "rep", None),
        P("ep", "rep", None),
    )
    return jax.shard_map(per_device, mesh=mesh, in_specs=in_specs, out_specs=out_specs, check_vma=False)
```

time: 633 us -> 206 us (0.33)
  waiting for transfers between devices: 480 us -> 0 us
  Pallas kernels: 0 us -> 197 us
  local copies, waits for them, and re-layouts: 75.8 us -> 1.76 us
  starting transfers between devices: 23.7 us -> 0 us
  matrix products: 20.6 us -> 0 us
  between operations: 14.3 us -> 0.68 us
  other arithmetic: 17.6 us -> 6.91 us
    pallas_call x0 -> x1, Pallas kernels: none -> 197 us  [exchange(): pl.pallas_call(functools.partial(outer, n_ep, n_rep), out_shape=(jax.Shap...]
    reduce_scatter x1 -> x0, waiting for transfers between devices: 171 us -> none  [per_device(): lax.psum_scatter(lax.dot_general(scaled, dout, (((0,), (0,)), ((), ())),...]
    all_to_all x3 -> x0, waiting for transfers between devices: 158 us -> none  [the longest x1 82.6 us: per_device(): lax.all_to_all(send_rows, 'ep', split_axis=0, concat_axis=0, tiled=True)]
    all_gather x1 -> x0, waiting for transfers between devices: 152 us -> none  [per_device(): lax.all_gather(master[0].astype(jnp.bfloat16), 'rep', axis=0, tiled=True)]
    gather x9 -> x0, local copies, waits for them, and re-layouts: 27.7 us -> none  [the longest x8 23.8 us: per_device(): back_pad[position[:, which]].astype(jnp.float32)]
    all_to_all x3 -> x0, starting transfers between devices: 23.4 us -> none  [the longest x1 10 us: per_device(): lax.all_to_all(send_weights, 'ep', split_axis=0, concat_axis=0, tiled=True)]
    scatter x2 -> x0, local copies, waits for them, and re-layouts: 22.6 us -> none  [the longest x1 14.6 us: per_device(): jnp.zeros((filled + 1,), gate_weights.dtype).at[flat_pos]]
    dot_general x3 -> x0, matrix products: 20.6 us -> none  [the longest x1 7.45 us: per_device(): jnp.dot(hidden, full_weight, preferred_element_type=jnp.float32)]
  transfers between devices with their start and end apart: 5 -> 0, of which waited for: 4 -> 0; matrix products, arithmetic and copies ran while one was open for 4% -> 0% of each run, Pallas kernels for 0% -> 0%
where the time goes in v1:
time: 206 us
  Pallas kernels  197 us (96%)
  other arithmetic  6.91 us (3%)
    pallas_call x1, Pallas kernels, exchange(): pl.pallas_call(functools.partial(outer, n_ep, n_rep), out_shape=(jax.Shap...  197 us
    convert_element_type x1, other arithmetic, adamw(): return (master_new, m_new.astype(jnp.bfloat16), v_new.astype(jnp.bfloat16))  5.63 us

profile of v1, /device:TPU:1, one launch (start us, length us, event | category | flops | bytes accessed | tf_op | source)
XLA Modules:
  0.0 206.2 jit_solution(3267418834935713771)
XLA Ops:
  0.6 1.3 convert_bitcast_fusion.gates_ref
  1.9 0.0 copy-start
  1.9 0.0 copy-start.2
  1.9 0.0 copy-start.3
  1.9 196.8 %exchange.1 = (bf16[384,2048]{1,0:T(8,128)(2,1)}, f32[8,256]{1,0:T(8,128)}, f32[128,3584]{1,0:T(8,128)}) custom-call(s32[8,256]{1,0:T(8,128)} %bitcast.25, s32[8,256]{1,0:T(8,128)} %bitcast.26, f32[8,256]{1,0:T(8,128)} %convert_bitcast_fusion.gates_ref, bf16[256,3584]{1,0:T(8,128)(2,1)} %og_hbm.1, bf16[384,2048]{1,0:T(8,128)(2,1)} %bitcast.24, ...), custom_call_target="tpu_custom_call" | custom-call | tf_op jit(solution)/shard_map/exchange/pallas_call | solution.py:476
  198.7 0.0 copy-done
  198.8 0.0 copy-done.2
  198.8 0.0 copy-done.3
  198.8 0.0 copy-start.1
  198.8 5.6 %fusion.3 = (bf16[1,128,3584]{2,1,0:T(8,128)(2,1)}, f32[1,128,3584]{2,1,0:T(8,128)}, bf16[1,128,3584]{2,1,0:T(8,128)(2,1)}) fusion(f32[128,3584]{1,0:T(8,128)} %get-tuple-element.10, bf16[1,128,3584]{2,1,0:T(8,128)(2,1)S(1)} %copy-done.2, f32[1,128,3584]{2,1,0:T(8,128)S(1)} %copy-done, bf16[1,128,3584]{2,1,0:T(8,128)(2,1)S(1)} %copy-done.3), kind=kLoop, calls=%fused_computation.6 | loop fusion | flops 8716288 | bytes 9175040 | tf_op jit(solution)/shard_map/convert_element_type | solution.py:33
  204.4 0.0 copy-start.4
  204.4 0.0 copy-done.1
  204.4 1.1 copy.15
  205.6 0.0 copy-done.4
  205.6 0.6 copy.16
Async XLA Ops:
  1.9 196.8 %copy-start = (f32[1,128,3584]{2,1,0:T(8,128)S(1)}, f32[1,128,3584]{2,1,0:T(8,128)}, u32[]{:S(2)}) copy-start(f32[1,128,3584]{2,1,0:T(8,128)} %param.13) | copy-start | bytes 5505028
  1.9 196.8 %copy-start.2 = (bf16[1,128,3584]{2,1,0:T(8,128)(2,1)S(1)}, bf16[1,128,3584]{2,1,0:T(8,128)(2,1)}, u32[]{:S(2)}) copy-start(bf16[1,128,3584]{2,1,0:T(8,128)(2,1)} %param.15) | copy-start | bytes 2752516
  1.9 196.8 %copy-start.3 = (bf16[1,128,3584]{2,1,0:T(8,128)(2,1)S(1)}, bf16[1,128,3584]{2,1,0:T(8,128)(2,1)}, u32[]{:S(2)}) copy-start(bf16[1,128,3584]{2,1,0:T(8,128)(2,1)} %param.14) | copy-start | bytes 2752516
  198.8 5.6 %copy-start.1 = (bf16[384,2048]{1,0:T(8,128)(2,1)S(1)}, bf16[384,2048]{1,0:T(8,128)(2,1)}, u32[]{:S(2)}) copy-start(bf16[384,2048]{1,0:T(8,128)(2,1)} %get-tuple-element.8) | copy-start | bytes 4718596
  204.4 1.1 copy-start.4

commit v2 on v1

--- a/solution.py
+++ b/solution.py
@@ -11,7 +11,7 @@
 EXP_LOCAL = 8
 SEND = 12
 PARTS = 4
-CHUNKS = (3, 4)
+CHUNKS = (2, 2, 1, 1, 1)
 TILE = 512
 MESH = pl.DeviceIdType.MESH
 
@@ -46,14 +46,14 @@
 
 def kernel(
     n_ep, n_rep,
-    ids_ref, slots_ref, gates_ref, og_hbm, gu_hbm, master_hbm,
-    ggu_out, gate_out, grad_out,
-    og, gu, master, pick, unpick,
+    ids_ref, slots_ref, gates_ref, og_hbm, gu_hbm, master_hbm, moment1_hbm, moment2_hbm,
+    ggu_out, gate_out, master_out, moment1_out, moment2_out,
+    og, gu, master, moment1, moment2, pick, unpick,
     rows_out, rows_in, w_out, w_in, dout, wcol,
     hidden, d_silu, silu, scaled_t, shards,
     s1, r1, keep, s2own, r2own, s2sum, r2sum, own, zs, zr,
     gg_acc, gg_out, gg_in,
-    load_sem, rows_ssem, rows_rsem, small_ssem, small_rsem, local_sem, ssem, rsem,
+    load_sem, store_sem, rows_ssem, rows_rsem, small_ssem, small_rsem, local_sem, ssem, rsem,
 ):
     f32, bf16 = jnp.float32, jnp.bfloat16
     r, e = lax.axis_index("rep"), lax.axis_index("ep")
@@ -73,7 +73,12 @@
 
     loads = [
         pltpu.make_async_copy(src, dst, load_sem.at[i])
-        for i, (src, dst) in enumerate(((og_hbm, og), (master_hbm, master), (gu_hbm, gu)))
+        for i, (src, dst) in enumerate(
+            (
+                (og_hbm, og), (master_hbm, master), (gu_hbm, gu),
+                (moment1_hbm, moment1), (moment2_hbm, moment2),
+            )
+        )
     ]
     for load in loads:
         load.start()
@@ -87,25 +92,50 @@
     lax.fori_loop(1, n_ep, greet, 0)
     for other in (up, down, across):
         pl.semaphore_signal(barrier, inc=1, device_id=other, device_id_type=MESH)
+
+    mine = pl.ds(pl.multiple_of(r * part_rows, part_rows), part_rows)
+    loads[1].wait()
+
+    def cast(t, _):
+        cols = pl.ds(pl.multiple_of(t * TILE, TILE), TILE)
+        shards[mine, cols] = master[:, cols].astype(bf16)
+        return _
+
+    lax.fori_loop(0, width // TILE, cast, 0)
+
+    def remote(src, dst, i, other):
+        return pltpu.make_async_remote_copy(
+            src_ref=src, dst_ref=dst, send_sem=ssem.at[i], recv_sem=rsem.at[i],
+            device_id=other, device_id_type=MESH,
+        )
+
+    pl.semaphore_wait(barrier, n_ep - 1 + 3)
+
+    def shard(rep):
+        return shards.at[pl.ds(pl.multiple_of(rep * part_rows, part_rows), part_rows)]
+
+    def half_shard(rep, which):
+        half = part_rows // 2
+        return shards.at[pl.ds(pl.multiple_of(rep * part_rows + which * half, half), half)]
+
+    started = []
+
+    def start(copy):
+        copy.start()
+        started.append(copy)
+        return copy
+
+    ag_up = start(remote(shard(r), shard(r), 0, up))
+    ag_down = start(remote(shard(r), shard(r), 1, down))
+    ag_z = start(remote(shard(r), shard(r), 4, across))
 
     ids, slots = ids_ref[...], slots_ref[...]
     live = ((ids & (EXP_LOCAL - 1)) == 0) & (slots >= 0)
     expert = ids >> 3
     pos12 = jnp.where(live, expert * SEND + slots, -64)
     pos16 = jnp.where(live, expert * 16 + slots, -64)
-    gates = gates_ref[...]
+    gates = gates_ref[...].astype(f32)
     n_tok = ids.shape[1]
-
-    def weight_rows(b, _):
-        row = iota((64, n_tok), 0) + b * 64
-        total = jnp.zeros((64, n_tok), f32)
-        for k in range(TOPK):
-            total += jnp.where(row == pos16[k : k + 1, :], gates[k : k + 1, :], 0.0)
-        column = jnp.sum(total, axis=1, keepdims=True)
-        w_out[pl.ds(pl.multiple_of(b * 64, 64), 64), :] = jnp.broadcast_to(column, (64, 128)).astype(bf16)
-        return _
-
-    lax.fori_loop(0, n_ep * 16 // 64, weight_rows, 0)
 
     def pick_rows(g, _):
         row = iota((PARTS * msg, n_tok), 0)
@@ -123,41 +153,6 @@
 
     lax.fori_loop(0, n_ep // PARTS, pick_rows, 0)
 
-    mine = pl.ds(pl.multiple_of(r * part_rows, part_rows), part_rows)
-    loads[1].wait()
-
-    def cast(t, _):
-        cols = pl.ds(pl.multiple_of(t * TILE, TILE), TILE)
-        shards[mine, cols] = master[:, cols].astype(bf16)
-        return _
-
-    lax.fori_loop(0, width // TILE, cast, 0)
-
-    def remote(src, dst, i, other):
-        return pltpu.make_async_remote_copy(
-            src_ref=src, dst_ref=dst, send_sem=ssem.at[i], recv_sem=rsem.at[i],
-            device_id=other, device_id_type=MESH,
-        )
-
-    pl.semaphore_wait(barrier, n_ep - 1 + 3)
-
-    def shard(rep):
-        return shards.at[pl.ds(pl.multiple_of(rep * part_rows, part_rows), part_rows)]
-
-    def half_shard(rep, which):
-        half = part_rows // 2
-        return shards.at[pl.ds(pl.multiple_of(rep * part_rows + which * half, half), half)]
-
-    started = []
-
-    def start(copy):
-        copy.start()
-        started.append(copy)
-        return copy
-
-    ag_up = start(remote(shard(r), shard(r), 0, up))
-    ag_down = start(remote(shard(r), shard(r), 1, down))
-
     def small(src_of, dst, rows, sems):
         def send(k, _):
             to = peer(k)
@@ -179,6 +174,16 @@
         part = ref.at[pl.ds(0, (n_ep - 1) * rows)]
         return pltpu.make_async_copy(part, part, sem)
 
+    def weight_rows(b, _):
+        row = iota((64, n_tok), 0) + b * 64
+        total = jnp.zeros((64, n_tok), f32)
+        for k in range(TOPK):
+            total += jnp.where(row == pos16[k : k + 1, :], gates[k : k + 1, :], 0.0)
+        column = jnp.sum(total, axis=1, keepdims=True)
+        w_out[pl.ds(pl.multiple_of(b * 64, 64), 64), :] = jnp.broadcast_to(column, (64, 128)).astype(bf16)
+        return _
+
+    lax.fori_loop(0, n_ep * 16 // 64, weight_rows, 0)
     w_local = small(lambda to: w_out.at[pl.ds(pl.multiple_of(to * 16, 16), 16)], w_in, 16, 0)
 
     loads[0].wait()
@@ -243,6 +248,11 @@
         iota((side, side), 1) == dest * msg + part * SEND + rest - dest * SEND, 1.0, 0.0
     ).astype(bf16)
 
+    ag_up.wait_recv()
+    ag_up2 = start(remote(half_shard(down[0], 0), half_shard(down[0], 0), 2, up))
+    ag_down.wait_recv()
+    ag_down2 = start(remote(half_shard(up[0], 1), half_shard(up[0], 1), 3, down))
+
     w_local.wait()
     all_of(w_in, 16, small_rsem.at[0]).wait()
     n_slots = n_ep * SEND
@@ -258,11 +268,6 @@
         return _
 
     lax.fori_loop(0, n_hidden // step, scale, 0)
-
-    ag_up.wait_recv()
-    ag_up2 = start(remote(half_shard(down[0], 0), half_shard(down[0], 0), 2, up))
-    ag_down.wait_recv()
-    ag_down2 = start(remote(half_shard(up[0], 1), half_shard(up[0], 1), 3, down))
 
     def span(p):
         return pl.ds(offsets[p], CHUNKS[p] * PARTS * 128)
@@ -339,32 +344,39 @@
             tiles(p, add)
             flights[p, "sum_" + name] = start(remote(s2sum.at[rows, span(p)], r2sum.at[rows, span(p)], j, other))
 
+    def half(which, cols):
+        rows = pl.ds(pl.multiple_of(which * part_rows, part_rows), part_rows)
+        return own[rows, cols] + (r2own[rows, cols].astype(f32) + r2sum[rows, cols].astype(f32))
+
     def stage_three(p):
         for name in ("own_a", "own_b", "sum_a", "sum_b"):
             flights[p, name].wait_recv()
 
-        def half(which, cols):
-            rows = pl.ds(pl.multiple_of(which * part_rows, part_rows), part_rows)
-            return own[rows, cols] + (r2own[rows, cols].astype(f32) + r2sum[rows, cols].astype(f32))
-
         def other(cols):
             zs[:, cols] = half(1 - h, cols).astype(bf16)
 
         tiles(p, other)
         flights[p, "z"] = start(remote(zs.at[:, span(p)], zr.at[:, span(p)], base + 7 * p + 6, across))
 
-        def mine_too(cols):
-            grad_out[:, cols] = half(h, cols)
-
-        tiles(p, mine_too)
+    stores = []
+
+    def store(src, dst):
+        copy = pltpu.make_async_copy(src, dst, store_sem.at[len(stores)])
+        copy.start()
+        stores.append(copy)
 
     def stage_four(p):
         flights[p, "z"].wait_recv()
 
         def finish(cols):
-            grad_out[:, cols] = grad_out[:, cols] + zr[:, cols].astype(f32)
+            grad = half(h, cols) + zr[:, cols].astype(f32)
+            master[:, cols], moment1[:, cols], moment2[:, cols] = adamw(
+                master[:, cols], moment1[:, cols], moment2[:, cols], grad
+            )
 
         tiles(p, finish)
+        for src, dst in ((master, master_out), (moment1, moment1_out), (moment2, moment2_out)):
+            store(src.at[:, span(p)], dst.at[:, span(p)])
 
     m_step = 128
 
@@ -384,40 +396,38 @@
                 total = total + felt[:, c * 128 : (c + 1) * 128]
             gg_acc[where, :] = total
             grad_hidden = wcol[where, 0:1] * proj
-            ggu_out[where, cols] = (grad_hidden * d_silu[where, cols]).astype(bf16)
-            ggu_out[where, up_cols] = (grad_hidden * silu[where, cols]).astype(bf16)
+            gu[where, cols] = (grad_hidden * d_silu[where, cols]).astype(bf16)
+            gu[where, up_cols] = (grad_hidden * silu[where, cols]).astype(bf16)
             return _
 
         lax.fori_loop(0, n_slots // m_step, block, 0)
 
     gg_acc[...] = jnp.zeros_like(gg_acc)
 
-    arrive(0)
-    stage_one(0)
-    ag_z = start(remote(shard(r), shard(r), 4, across))
-    stage_two(0)
-    arrive(1)
-    stage_one(1)
-    stage_three(0)
-    stage_two(1)
-
+    up_other, down_other = lax.rem(across[0] + 2, n_rep), lax.rem(across[0] + n_rep - 2, n_rep)
     ag_z.wait_recv()
     ag_up3 = start(remote(shard(across[0]), shard(across[0]), 5, up))
     ag_down3 = start(remote(shard(across[0]), shard(across[0]), 6, down))
-    stage_three(1)
-    gate_part(y)
-    up_other, down_other = across[0] + 2, across[0] + n_rep - 2
-    up_other, down_other = lax.rem(up_other, n_rep), lax.rem(down_other, n_rep)
     ag_up3.wait_recv()
     ag_up4 = start(remote(half_shard(down_other, 0), half_shard(down_other, 0), 7, up))
     ag_down3.wait_recv()
     ag_down4 = start(remote(half_shard(up_other, 1), half_shard(up_other, 1), 8, down))
+
+    last = len(CHUNKS) - 1
+    for p in range(last + 1):
+        arrive(p)
+        stage_one(p)
+        if p:
+            stage_three(p - 1)
+        stage_two(p)
+    gate_part(y)
     gate_part(y_down)
     gate_part(y_up)
-    stage_four(0)
     for copy in (ag_up2, ag_down2, ag_up4, ag_down4):
         copy.wait_recv()
     gate_part(y_far)
+    store(gu, ggu_out)
+    stage_three(last)
 
     gg_out[...] = jnp.broadcast_to(jnp.sum(gg_acc[...], axis=1, keepdims=True), gg_out.shape)
 
@@ -425,7 +435,10 @@
         return gg_out.at[pl.ds(pl.multiple_of(to * SEND - 4 * lax.rem(to, 2), 8), 16)]
 
     gg_local = small(window, gg_in, 16, 1)
-    stage_four(1)
+    loads[3].wait()
+    loads[4].wait()
+    for p in range(last + 1):
+        stage_four(p)
     gg_local.wait()
     all_of(gg_in, 16, small_rsem.at[1]).wait()
     row = iota((n_ep * 16, 128), 0) - 4 * lax.rem(e, 2)
@@ -436,6 +449,8 @@
             hit = row == pos16[k : k + 1, cols]
             gate_out[k : k + 1, cols] = jnp.sum(jnp.where(hit, back, 0.0), axis=0, keepdims=True)
 
+    for copy in stores:
+        copy.wait()
     for copy in started:
         copy.wait_send()
     all_of(w_out, 16, small_ssem.at[0]).wait()
@@ -446,20 +461,19 @@
 
 def outer(
     n_ep, n_rep,
-    ids_ref, slots_ref, gates_ref, og_hbm, gu_hbm, master_hbm,
-    ggu_out, gate_out, grad_out, *scratch,
+    ids_ref, slots_ref, gates_ref, og_hbm, gu_hbm, master_hbm, moment1_hbm, moment2_hbm,
+    ggu_out, gate_out, master_out, moment1_out, moment2_out, *scratch,
 ):
     n = len(CHUNKS)
-    og, gu, master, pick, unpick = scratch[:5]
-    rows_out, rows_in = scratch[5 : 5 + n], scratch[5 + n : 5 + 2 * n]
+    rows_out, rows_in = scratch[7 : 7 + n], scratch[7 + n : 7 + 2 * n]
     kernel(
-        n_ep, n_rep, ids_ref, slots_ref, gates_ref, og_hbm, gu_hbm, master_hbm,
-        ggu_out, gate_out, grad_out,
-        og, gu, master, pick, unpick, rows_out, rows_in, *scratch[5 + 2 * n :],
+        n_ep, n_rep, ids_ref, slots_ref, gates_ref, og_hbm, gu_hbm, master_hbm, moment1_hbm, moment2_hbm,
+        ggu_out, gate_out, master_out, moment1_out, moment2_out,
+        *scratch[:7], rows_out, rows_in, *scratch[7 + 2 * n :],
     )
 
 
-def exchange(n_ep, n_rep, ids, slots, gates, out_grad, gate_up, master):
+def exchange(n_ep, n_rep, ids, slots, gates, out_grad, gate_up, master, moment1, moment2):
     tokens, width = out_grad.shape
     n_slots, two_hidden = gate_up.shape
     n_hidden = two_hidden // 2
@@ -479,13 +493,17 @@
             jax.ShapeDtypeStruct((n_slots, two_hidden), bf16),
             jax.ShapeDtypeStruct((TOPK, tokens), f32),
             jax.ShapeDtypeStruct((part_rows, width), f32),
+            jax.ShapeDtypeStruct((part_rows, width), bf16),
+            jax.ShapeDtypeStruct((part_rows, width), bf16),
         ),
-        in_specs=[vmem, vmem, vmem, hbm, hbm, hbm],
-        out_specs=(vmem, vmem, vmem),
+        in_specs=[vmem, vmem, vmem, hbm, hbm, hbm, hbm, hbm],
+        out_specs=(hbm, vmem, hbm, hbm, hbm),
         scratch_shapes=[
             pltpu.VMEM((tokens, width), bf16),
             pltpu.VMEM((n_slots, two_hidden), bf16),
             pltpu.VMEM((part_rows, width), f32),
+            pltpu.VMEM((part_rows, width), bf16),
+            pltpu.VMEM((part_rows, width), bf16),
             pltpu.VMEM((n_ep * msg, PARTS * tokens), bf16),
             pltpu.VMEM((PARTS * msg, PARTS * msg), bf16),
             *rows,
@@ -512,7 +530,8 @@
             pltpu.VMEM((n_slots, 128), f32),
             pltpu.VMEM((n_slots, 128), f32),
             pltpu.VMEM((n_ep * 16, 128), f32),
-            dma((3,)),
+            dma((5,)),
+            dma((1 + 3 * n,)),
             dma((n,)),
             dma((n,)),
             dma((2,)),
@@ -525,19 +544,49 @@
             collective_id=0, has_side_effects=True, vmem_limit_bytes=60 * 1024 * 1024
         ),
         name="exchange",
-    )(ids, slots, gates, out_grad, gate_up, master)
+    )(ids, slots, gates, out_grad, gate_up, master, moment1, moment2)
+
+
+def hand_over(n, *refs):
+    given, taken, held = refs[:n], refs[n : 2 * n], refs[2 * n : 3 * n]
+    get_sem, put_sem = refs[3 * n :]
+    gets = [pltpu.make_async_copy(given[i], held[i], get_sem.at[i]) for i in range(n)]
+    puts = [pltpu.make_async_copy(held[i], taken[i], put_sem.at[i]) for i in range(n)]
+    for get in gets:
+        get.start()
+    for get, put in zip(gets, puts):
+        get.wait()
+        put.start()
+    for put in puts:
+        put.wait()
+
+
+def results(*arrays):
+    n = len(arrays)
+    hbm = pl.BlockSpec(memory_space=pl.ANY)
+    sems = pltpu.SemaphoreType.DMA((n,))
+    return pl.pallas_call(
+        functools.partial(hand_over, n),
+        out_shape=tuple(jax.ShapeDtypeStruct(a.shape, a.dtype) for a in arrays),
+        in_specs=[hbm] * n,
+        out_specs=(hbm,) * n,
+        scratch_shapes=[*(pltpu.VMEM(a.shape, a.dtype) for a in arrays), sems, sems],
+        compiler_params=pltpu.CompilerParams(vmem_limit_bytes=62 * 1024 * 1024),
+        name="results",
+    )(*arrays)
 
 
 def solution(mesh):
     n_ep, n_rep = mesh.shape["ep"], mesh.shape["rep"]
 
     def per_device(out_grad, expert_ids, slots, gate_weights, saved_gate_up, master, moment1, moment2):
-        grad_gate_up, gate_grad, grad = exchange(
-            n_ep, n_rep, expert_ids.T, slots.T, gate_weights.T.astype(jnp.float32),
-            out_grad, saved_gate_up[0, 0], master[0],
+        grad_gate_up, gate_grad, *state = results(
+            *exchange(
+                n_ep, n_rep, expert_ids.T, slots.T, gate_weights.T,
+                out_grad, saved_gate_up[0, 0], master[0], moment1[0], moment2[0],
+            )
         )
-        master_out, moment1_out, moment2_out = adamw(master, moment1, moment2, grad[None])
-        return (grad_gate_up.reshape(saved_gate_up.shape), gate_grad.T, master_out, moment1_out, moment2_out)
+        return (grad_gate_up.reshape(saved_gate_up.shape), gate_grad.T, *(part[None] for part in state))
 
     in_specs = (
         P(("rep", "ep"), None),

time: 206 us -> 174 us (0.84)
  Pallas kernels: 197 us -> 173 us
  other arithmetic: 6.91 us -> 0 us
    pallas_call x1, Pallas kernels: 197 us -> 169 us  [exchange(): pl.pallas_call(functools.partial(outer, n_ep, n_rep), out_shape=(jax.Shap...]
    convert_element_type x2 -> x0, other arithmetic: 6.91 us -> none  [the longest x1 5.63 us: adamw(): return (master_new, m_new.astype(jnp.bfloat16), v_new.astype(jnp.bfloat16))]
    pallas_call x0 -> x1, Pallas kernels: none -> 3.91 us  [results(): pl.pallas_call(functools.partial(hand_over, n), out_shape=tuple((jax.Shap...]
where the time goes in v2:
time: 174 us
  Pallas kernels  173 us (99%)
    pallas_call x1, Pallas kernels, exchange(): pl.pallas_call(functools.partial(outer, n_ep, n_rep), out_shape=(jax.Shap...  169 us
    pallas_call x1, Pallas kernels, results(): pl.pallas_call(functools.partial(hand_over, n), out_shape=tuple((jax.Shap...  3.91 us

profile of v2, /device:TPU:1, one launch (start us, length us, event | category | flops | bytes accessed | tf_op | source)
XLA Modules:
  0.0 173.7 jit_solution(16814812260825091486)
XLA Ops:
  0.6 169.2 %exchange.1 = (bf16[384,2048]{1,0:T(8,128)(2,1)}, f32[8,256]{1,0:T(8,128)}, f32[128,3584]{1,0:T(8,128)}, bf16[128,3584]{1,0:T(8,128)(2,1)}, bf16[128,3584]{1,0:T(8,128)(2,1)}) custom-call(s32[8,256]{1,0:T(8,128)} %bitcast.16, s32[8,256]{1,0:T(8,128)} %bitcast.17, bf16[8,256]{1,0:T(8,128)(2,1)} %bitcast.18, bf16[256,3584]{1,0:T(8,128)(2,1)} %og_hbm.1, ...), custom_call_target="tpu_custom_call" | custom-call | tf_op jit(solution)/shard_map/exchange/pallas_call | solution.py:490
  169.8 3.9 %results.1 = (bf16[384,2048]{1,0:T(8,128)(2,1)}, f32[8,256]{1,0:T(8,128)}, f32[128,3584]{1,0:T(8,128)}, bf16[128,3584]{1,0:T(8,128)(2,1)}, bf16[128,3584]{1,0:T(8,128)(2,1)}) custom-call(bf16[384,2048]{1,0:T(8,128)(2,1)} %get-tuple-element.15.refs_0_, f32[8,256]{1,0:T(8,128)} %get-tuple-element.16.refs_1_, f32[128,3584]{1,0:T(8,128)} %get-tuple-element.17.refs_2_, ...), custom_call_target="tpu_custom_call" | custom-call | tf_op jit(solution)/shard_map/results/pallas_call | solution.py:568

commit v3 on v2

--- a/solution.py
+++ b/solution.py
@@ -50,7 +50,7 @@
     ggu_out, gate_out, master_out, moment1_out, moment2_out,
     og, gu, master, moment1, moment2, pick, unpick,
     rows_out, rows_in, w_out, w_in, dout, wcol,
-    hidden, d_silu, silu, scaled_t, shards,
+    hidden, d_silu, silu, proj, scaled_t, shards,
     s1, r1, keep, s2own, r2own, s2sum, r2sum, own, zs, zr,
     gg_acc, gg_out, gg_in,
     load_sem, store_sem, rows_ssem, rows_rsem, small_ssem, small_rsem, local_sem, ssem, rsem,
@@ -80,8 +80,7 @@
             )
         )
     ]
-    for load in loads:
-        load.start()
+    loads[1].start()
 
     barrier = pltpu.get_barrier_semaphore()
 
@@ -109,6 +108,8 @@
             device_id=other, device_id_type=MESH,
         )
 
+    for i in (0, 2, 3, 4):
+        loads[i].start()
     pl.semaphore_wait(barrier, n_ep - 1 + 3)
 
     def shard(rep):
@@ -378,29 +379,29 @@
         for src, dst in ((master, master_out), (moment1, moment1_out), (moment2, moment2_out)):
             store(src.at[:, span(p)], dst.at[:, span(p)])
 
-    m_step = 128
-
-    def gate_part(to_y):
-        rows = pl.ds(pl.multiple_of(to_y * pair, pair), pair)
-        cols = rows
-        up_cols = pl.ds(pl.multiple_of(n_hidden + to_y * pair, pair), pair)
-
-        def block(m, _):
-            where = pl.ds(pl.multiple_of(m * m_step, m_step), m_step)
-            proj = lax.dot_general(
-                dout[where, :], shards[rows, :], (((1,), (1,)), ((), ())), preferred_element_type=f32
+    def project(p):
+        def block(b, _):
+            rows = pl.ds(pl.multiple_of(b * pair, pair), pair)
+            got = lax.dot_general(
+                dout[:, span(p)], shards[rows, span(p)], (((1,), (1,)), ((), ())), preferred_element_type=f32
             )
-            felt = hidden[where, cols].astype(f32) * proj
-            total = gg_acc[where, :]
-            for c in range(pair // 128):
-                total = total + felt[:, c * 128 : (c + 1) * 128]
-            gg_acc[where, :] = total
-            grad_hidden = wcol[where, 0:1] * proj
-            gu[where, cols] = (grad_hidden * d_silu[where, cols]).astype(bf16)
-            gu[where, up_cols] = (grad_hidden * silu[where, cols]).astype(bf16)
+            proj[:, rows] = got if p == 0 else proj[:, rows] + got
             return _
 
-        lax.fori_loop(0, n_slots // m_step, block, 0)
+        lax.fori_loop(0, n_hidden // pair, block, 0)
+
+    def gate_finish():
+        def block(t, _):
+            cols = pl.ds(pl.multiple_of(t * step, step), step)
+            up_cols = pl.ds(pl.multiple_of(n_hidden + t * step, step), step)
+            value = proj[:, cols]
+            gg_acc[...] += hidden[:, cols].astype(f32) * value
+            grad_hidden = wcol[...] * value
+            gu[:, cols] = (grad_hidden * d_silu[:, cols]).astype(bf16)
+            gu[:, up_cols] = (grad_hidden * silu[:, cols]).astype(bf16)
+            return _
+
+        lax.fori_loop(0, n_hidden // step, block, 0)
 
     gg_acc[...] = jnp.zeros_like(gg_acc)
 
@@ -420,12 +421,11 @@
         if p:
             stage_three(p - 1)
         stage_two(p)
-    gate_part(y)
-    gate_part(y_down)
-    gate_part(y_up)
-    for copy in (ag_up2, ag_down2, ag_up4, ag_down4):
-        copy.wait_recv()
-    gate_part(y_far)
+        if p == 0:
+            for copy in (ag_up2, ag_down2, ag_up4, ag_down4):
+                copy.wait_recv()
+        project(p)
+    gate_finish()
     store(gu, ggu_out)
     stage_three(last)
 
@@ -437,7 +437,7 @@
     gg_local = small(window, gg_in, 16, 1)
     loads[3].wait()
     loads[4].wait()
-    for p in range(last + 1):
+    for p in range(last):
         stage_four(p)
     gg_local.wait()
     all_of(gg_in, 16, small_rsem.at[1]).wait()
@@ -449,6 +449,7 @@
             hit = row == pos16[k : k + 1, cols]
             gate_out[k : k + 1, cols] = jnp.sum(jnp.where(hit, back, 0.0), axis=0, keepdims=True)
 
+    stage_four(last)
     for copy in stores:
         copy.wait()
     for copy in started:
@@ -515,6 +516,7 @@
             pltpu.VMEM((n_slots, n_hidden), bf16),
             pltpu.VMEM((n_slots, n_hidden), f32),
             pltpu.VMEM((n_slots, n_hidden), f32),
+            pltpu.VMEM((n_slots, n_hidden), f32),
             pltpu.VMEM((n_hidden, n_slots), bf16),
             pltpu.VMEM((n_hidden, width), bf16),
             pltpu.VMEM((pair, width), bf16),

time: 174 us -> 172 us (0.989)
  Pallas kernels: 173 us -> 171 us
where the time goes in v3:
time: 172 us
  Pallas kernels  171 us (99%)
    pallas_call x1, Pallas kernels, exchange(): pl.pallas_call(functools.partial(outer, n_ep, n_rep), out_shape=(jax.Shap...  167 us
    pallas_call x1, Pallas kernels, results(): pl.pallas_call(functools.partial(hand_over, n), out_shape=tuple((jax.Shap...  3.91 us

profile of v3, /device:TPU:1, one launch (start us, length us, event | category | flops | bytes accessed | tf_op | source)
XLA Modules:
  0.0 172.0 jit_solution(5871211563008083996)
XLA Ops:
  0.6 167.4 %exchange.1 = (bf16[384,2048]{1,0:T(8,128)(2,1)}, f32[8,256]{1,0:T(8,128)}, f32[128,3584]{1,0:T(8,128)}, bf16[128,3584]{1,0:T(8,128)(2,1)}, bf16[128,3584]{1,0:T(8,128)(2,1)}) custom-call(s32[8,256]{1,0:T(8,128)} %bitcast.16, s32[8,256]{1,0:T(8,128)} %bitcast.17, bf16[8,256]{1,0:T(8,128)(2,1)} %bitcast.18, bf16[256,3584]{1,0:T(8,128)(2,1)} %og_hbm.1, ...), custom_call_target="tpu_custom_call" | custom-call | tf_op jit(solution)/shard_map/exchange/pallas_call | solution.py:491
  168.1 3.9 %results.1 = (bf16[384,2048]{1,0:T(8,128)(2,1)}, f32[8,256]{1,0:T(8,128)}, f32[128,3584]{1,0:T(8,128)}, bf16[128,3584]{1,0:T(8,128)(2,1)}, bf16[128,3584]{1,0:T(8,128)(2,1)}) custom-call(bf16[384,2048]{1,0:T(8,128)(2,1)} %get-tuple-element.15.refs_0_, f32[8,256]{1,0:T(8,128)} %get-tuple-element.16.refs_1_, f32[128,3584]{1,0:T(8,128)} %get-tuple-element.17.refs_2_, ...), custom_call_target="tpu_custom_call" | custom-call | tf_op jit(solution)/shard_map/results/pallas_call | solution.py:570

commit v4 on v3

--- a/solution.py
+++ b/solution.py
@@ -211,7 +211,7 @@
             return ref.at[pl.ds(pl.multiple_of(i * msg, 16), msg)]
 
         def send(k, _, out=out, into=into, p=p):
-            to = peer(k)
+            to = peer(k * 5)
             pltpu.make_async_remote_copy(
                 src_ref=block(out, to), dst_ref=block(into, e),
                 send_sem=rows_ssem.at[p], recv_sem=rows_rsem.at[p],
@@ -552,8 +552,9 @@
 def hand_over(n, *refs):
     given, taken, held = refs[:n], refs[n : 2 * n], refs[2 * n : 3 * n]
     get_sem, put_sem = refs[3 * n :]
-    gets = [pltpu.make_async_copy(given[i], held[i], get_sem.at[i]) for i in range(n)]
-    puts = [pltpu.make_async_copy(held[i], taken[i], put_sem.at[i]) for i in range(n)]
+    largest_first = sorted(range(n), key=lambda i: -given[i].size * given[i].dtype.itemsize)
+    gets = [pltpu.make_async_copy(given[i], held[i], get_sem.at[i]) for i in largest_first]
+    puts = [pltpu.make_async_copy(held[i], taken[i], put_sem.at[i]) for i in largest_first]
     for get in gets:
         get.start()
     for get, put in zip(gets, puts):

time: 172 us -> 172 us (level)
  no operation moved by 1% of the time
where the time goes in v4:
time: 172 us
  Pallas kernels  171 us (99%)
    pallas_call x1, Pallas kernels, exchange(): pl.pallas_call(functools.partial(outer, n_ep, n_rep), out_shape=(jax.Shap...  167 us
    pallas_call x1, Pallas kernels, results(): pl.pallas_call(functools.partial(hand_over, n), out_shape=tuple((jax.Shap...  3.94 us

profile of v4, /device:TPU:1, one launch (start us, length us, event | category | flops | bytes accessed | tf_op | source)
XLA Modules:
  0.0 171.9 jit_solution(2912756639804270526)
XLA Ops:
  0.6 167.3 %exchange.1 = (bf16[384,2048]{1,0:T(8,128)(2,1)}, f32[8,256]{1,0:T(8,128)}, f32[128,3584]{1,0:T(8,128)}, bf16[128,3584]{1,0:T(8,128)(2,1)}, bf16[128,3584]{1,0:T(8,128)(2,1)}) custom-call(s32[8,256]{1,0:T(8,128)} %bitcast.16, s32[8,256]{1,0:T(8,128)} %bitcast.17, bf16[8,256]{1,0:T(8,128)(2,1)} %bitcast.18, bf16[256,3584]{1,0:T(8,128)(2,1)} %og_hbm.1, ...), custom_call_target="tpu_custom_call" | custom-call | tf_op jit(solution)/shard_map/exchange/pallas_call | solution.py:491
  168.0 3.9 %results.1 = (bf16[384,2048]{1,0:T(8,128)(2,1)}, f32[8,256]{1,0:T(8,128)}, f32[128,3584]{1,0:T(8,128)}, bf16[128,3584]{1,0:T(8,128)(2,1)}, bf16[128,3584]{1,0:T(8,128)(2,1)}) custom-call(bf16[384,2048]{1,0:T(8,128)(2,1)} %get-tuple-element.15.refs_0_, f32[8,256]{1,0:T(8,128)} %get-tuple-element.16.refs_1_, f32[128,3584]{1,0:T(8,128)} %get-tuple-element.17.refs_2_, ...), custom_call_target="tpu_custom_call" | custom-call | tf_op jit(solution)/shard_map/results/pallas_call | solution.py:571

commit v5 on v3

--- a/solution.py
+++ b/solution.py
@@ -126,9 +126,9 @@
         started.append(copy)
         return copy
 
+    ag_z = start(remote(shard(r), shard(r), 4, across))
     ag_up = start(remote(shard(r), shard(r), 0, up))
     ag_down = start(remote(shard(r), shard(r), 1, down))
-    ag_z = start(remote(shard(r), shard(r), 4, across))
 
     ids, slots = ids_ref[...], slots_ref[...]
     live = ((ids & (EXP_LOCAL - 1)) == 0) & (slots >= 0)
@@ -424,7 +424,9 @@
         if p == 0:
             for copy in (ag_up2, ag_down2, ag_up4, ag_down4):
                 copy.wait_recv()
-        project(p)
+        if p:
+            project(p - 1)
+    project(last)
     gate_finish()
     store(gu, ggu_out)
     stage_three(last)

time: 172 us -> 172 us (level)
  no operation moved by 1% of the time
where the time goes in v5:
time: 172 us
  Pallas kernels  171 us (99%)
    pallas_call x1, Pallas kernels, exchange(): pl.pallas_call(functools.partial(outer, n_ep, n_rep), out_shape=(jax.Shap...  167 us
    pallas_call x1, Pallas kernels, results(): pl.pallas_call(functools.partial(hand_over, n), out_shape=tuple((jax.Shap...  3.91 us

profile of v5, /device:TPU:1, one launch (start us, length us, event | category | flops | bytes accessed | tf_op | source)
XLA Modules:
  0.0 171.9 jit_solution(17240239168584119583)
XLA Ops:
  0.6 167.4 %exchange.1 = (bf16[384,2048]{1,0:T(8,128)(2,1)}, f32[8,256]{1,0:T(8,128)}, f32[128,3584]{1,0:T(8,128)}, bf16[128,3584]{1,0:T(8,128)(2,1)}, bf16[128,3584]{1,0:T(8,128)(2,1)}) custom-call(s32[8,256]{1,0:T(8,128)} %bitcast.16, s32[8,256]{1,0:T(8,128)} %bitcast.17, bf16[8,256]{1,0:T(8,128)(2,1)} %bitcast.18, bf16[256,3584]{1,0:T(8,128)(2,1)} %og_hbm.1, ...), custom_call_target="tpu_custom_call" | custom-call | tf_op jit(solution)/shard_map/exchange/pallas_call | solution.py:493
  168.0 3.9 %results.1 = (bf16[384,2048]{1,0:T(8,128)(2,1)}, f32[8,256]{1,0:T(8,128)}, f32[128,3584]{1,0:T(8,128)}, bf16[128,3584]{1,0:T(8,128)(2,1)}, bf16[128,3584]{1,0:T(8,128)(2,1)}) custom-call(bf16[384,2048]{1,0:T(8,128)(2,1)} %get-tuple-element.15.refs_0_, f32[8,256]{1,0:T(8,128)} %get-tuple-element.16.refs_1_, f32[128,3584]{1,0:T(8,128)} %get-tuple-element.17.refs_2_, ...), custom_call_target="tpu_custom_call" | custom-call | tf_op jit(solution)/shard_map/results/pallas_call | solution.py:572
